TPU v7x, 32 devices: a whole 2x2x4 slice. The times are simulated.
32 devices in a mesh: groups: 2 (over x), lon: 16 (over z, y, core).
Axes of the slice: x: 2, y: 2, z: 4, core: 2. Of those that a mesh axis runs over, the one named last changes fastest.
Arguments:
- tokens: bfloat16 [64, 96, 512], P('groups', 'lon'), parts along dimension 0, may hold values from -36 to 36
- input_weight: bfloat16 [512, 1536], replicated, may hold values from -0.25 to 0.25
- output_weight: bfloat16 [512, 512], replicated, may hold values from -0.25 to 0.25
- upstream: bfloat16 [64, 96, 512], P('groups', 'lon'), parts along dimension 0, may hold values from -6 to 6
Outputs:
- token_grads: bfloat16 [64, 96, 512], P('groups', 'lon'), parts along dimension 0
- input_grads: float32 [512, 3072], P('lon', 'groups'), parts along dimension 1
- output_grads: float32 [1024, 512], P('groups', 'lon'), parts along dimension 0
There are 2 independent parts, one for each index of `groups`. A program takes and returns all parts, laid end to end along the dimension named above; an argument that names none is the same for every part. Nothing has to cross between parts.
All inputs are finite; a program needn't handle non-finite values.
Results may differ from a plain program's by a relative error of at most 0.005.
The roundings to bfloat16 on the way count: a program that leaves them out, or rounds other values in their place, can miss the bound.
Values may be sent and summed in bfloat16 or wider, within the bound.
A program may use at most 64 MiB of HBM per device.

v0:
```python
import jax
import jax.numpy as jnp
from jax import lax
from jax.sharding import PartitionSpec as P

HEADS = 8
RADIUS = 10


def from_behind(array, axis, by):
    size = lax.axis_size(axis)
    return lax.ppermute(array, axis, [(i, (i + by) % size) for i in range(size)])


def window_mask(lat_rows, cols, wide):
    query_lat = jnp.repeat(jnp.arange(lat_rows), cols)
    query_col = jnp.tile(jnp.arange(cols), lat_rows)
    key_lat = jnp.repeat(jnp.arange(lat_rows), wide)
    key_col = jnp.tile(jnp.arange(wide), lat_rows)
    near_lat = jnp.abs(query_lat[:, None] - key_lat[None, :]) <= RADIUS
    near_col = jnp.abs(query_col[:, None] + RADIUS - key_col[None, :]) <= RADIUS
    return near_lat & near_col


def rim_widths(cols):
    hop_count = (RADIUS + cols - 1) // cols
    return [min(cols, RADIUS - (distance - 1) * cols) for distance in range(1, hop_count + 1)]


def reach(block, send):
    cols = block.shape[2]
    widths = rim_widths(cols)
    left_parts = []
    right_parts = []
    for distance in range(1, len(widths) + 1):
        count = widths[distance - 1]
        left_parts.insert(0, send(block[:, :, cols - count :], distance))
        right_parts.append(send(block[:, :, :count], -distance))
    return jnp.concatenate(left_parts + [block] + right_parts, axis=2)


def give_back(extended, send):
    cols = extended.shape[2] - 2 * RADIUS
    widths = rim_widths(cols)
    hop_count = len(widths)
    own_part = extended[:, :, RADIUS : RADIUS + cols]
    left_pieces = []
    right_pieces = []
    for distance in range(1, hop_count + 1):
        count = widths[distance - 1]
        left_start = RADIUS - (distance - 1) * cols - count
        right_start = RADIUS + cols + (distance - 1) * cols
        left_pieces.append(extended[:, :, left_start : left_start + count])
        right_pieces.append(extended[:, :, right_start : right_start + count])
    for distance in range(1, hop_count + 1):
        count = widths[distance - 1]
        own_part = own_part.at[:, :, cols - count :].add(send(left_pieces[distance - 1], -distance))
        own_part = own_part.at[:, :, :count].add(send(right_pieces[distance - 1], distance))
    return own_part


def contract_rows(left_side, right_side):
    return lax.dot_general(
        left_side, right_side, (((1,), (1,)), ((), ())), preferred_element_type=jnp.float32
    )


def contract_first(left_side, right_side):
    return lax.dot_general(
        left_side, right_side, (((0,), (0,)), ((), ())), preferred_element_type=jnp.float32
    )


def attend(items, mask, scale):
    query_head, key_head, value_head, grad_head = items
    score = scale * contract_rows(query_head, key_head)
    score = jnp.where(mask, score, -jnp.inf)
    peak = jnp.max(score, axis=1, keepdims=True)
    lse = peak[:, 0] + jnp.log(jnp.sum(jnp.exp(score - peak), axis=1))
    probs = jnp.exp(score - lse[:, None])
    probs_low = probs.astype(jnp.bfloat16)
    attended = jnp.dot(probs_low, value_head, preferred_element_type=jnp.float32).astype(
        jnp.bfloat16
    )
    delta = jnp.sum(grad_head.astype(jnp.float32) * attended.astype(jnp.float32), axis=1)
    grad_probs = contract_rows(grad_head, value_head)
    grad_score = (probs * (grad_probs - delta[:, None])).astype(jnp.bfloat16)
    grad_query = scale * jnp.dot(grad_score, key_head, preferred_element_type=jnp.float32)
    grad_key = scale * contract_first(grad_score, query_head)
    grad_value = contract_first(probs_low, grad_head)
    return (attended, lse, delta, grad_query, grad_key, grad_value)


def body(tokens, input_weight, output_weight, upstream):
    lat_rows, cols, width = tokens.shape
    head_dim = width // HEADS
    wide = cols + 2 * RADIUS
    scale = head_dim ** (-0.5)
    flat = tokens.reshape(lat_rows * cols, width)
    projected = jnp.dot(flat, input_weight, preferred_element_type=jnp.float32).astype(jnp.bfloat16)
    query_all = projected[:, :width]
    key_all = projected[:, width : 2 * width]
    value_all = projected[:, 2 * width :]
    grad_flat = upstream.reshape(lat_rows * cols, width)
    grad_attn = contract_rows(grad_flat, output_weight).astype(jnp.bfloat16)

    def split_heads(array):
        return array.reshape(array.shape[0], HEADS, head_dim).transpose(1, 0, 2)

    def join_heads(array):
        return array.transpose(1, 0, 2).reshape(array.shape[1], HEADS * head_dim)

    pairs = jnp.stack([key_all, value_all]).reshape(2, lat_rows, cols, width)
    pairs_ext = reach(pairs, lambda piece, distance: from_behind(piece, "lon", distance))
    pairs_ext = pairs_ext.reshape(2, lat_rows * wide, width)
    mask = window_mask(lat_rows, cols, wide)
    results = lax.map(
        lambda items: attend(items, mask, scale),
        (
            split_heads(query_all),
            split_heads(pairs_ext[0]),
            split_heads(pairs_ext[1]),
            split_heads(grad_attn),
        ),
    )
    attended, lse, delta, grad_query, grad_key_ext, grad_value_ext = results
    partial_ext = jnp.stack([join_heads(grad_key_ext), join_heads(grad_value_ext)]).reshape(
        2, lat_rows, wide, width
    )
    returned = give_back(partial_ext, lambda piece, distance: from_behind(piece, "lon", distance))
    grad_key = returned[0].reshape(lat_rows * cols, width)
    grad_value = returned[1].reshape(lat_rows * cols, width)
    combined = jnp.concatenate([join_heads(grad_query), grad_key, grad_value], axis=1).astype(
        jnp.bfloat16
    )
    token_grads = (
        contract_rows(combined, input_weight).astype(jnp.bfloat16).reshape(lat_rows, cols, width)
    )
    attended_flat = join_heads(attended)
    term_input = contract_first(flat, combined)
    term_output = contract_first(attended_flat, grad_flat)
    input_grads, output_grads = (
        lax.psum_scatter(term_input, "lon", scatter_dimension=0, tiled=True),
        lax.psum_scatter(term_output, "lon", scatter_dimension=1, tiled=True),
    )
    return (token_grads, input_grads, output_grads)


def solution(mesh):
    in_specs = (P("groups", "lon", None), P(), P(), P("groups", "lon", None))
    out_specs = (P("groups", "lon", None), P("lon", "groups"), P("groups", "lon"))
    return jax.shard_map(body, mesh=mesh, in_specs=in_specs, out_specs=out_specs, check_vma=False)
```

profile of v0, /device:TPU:0, one launch (start us, length us, event | category | flops | bytes accessed | tf_op | source)
XLA Modules:
  0.0 302.1 jit_solution(7499166169675615086)
XLA Ops:
  9.5 5.5 %collective-permute-start.2 = (bf16[2,32,6,512]{3,2,1,0:T(8,128)(2,1)S(1)}, bf16[2,32,6,512]{3,2,1,0:T(8,128)(2,1)}, u32[]{:S(2)}, u32[]{:S(2)}) collective-permute-start(bf16[2,32,6,512]{3,2,1,0:T(8,128)(2,1)S(1)} %constant_dynamic-update-slice_fusion), channel_id=1, source_target_pairs={{0,15},{1,0},{2,1},{3,2},{4,3},{5,4},{6,5},{7,6},{8,7},{9,8},{10,9... | collective-permute-start | bytes 1179656 | tf_op jit(solution)/shard_map/ppermute | solution.py:12
  20.0 16.6 %collective-permute-done.3 = bf16[2,32,4,512]{3,2,1,0:T(4,128)(2,1)} collective-permute-done((bf16[2,32,4,512]{3,2,1,0:T(4,128)(2,1)}, bf16[2,32,4,512]{3,2,1,0:T(4,128)(2,1)}, u32[]{:S(2)}, u32[]{:S(2)}) %collective-permute-start.3) | collective-permute-done | bytes 262176 | tf_op jit(solution)/shard_map/ppermute | solution.py:12
  36.6 28.2 %concatenate.17 = bf16[2,32,26,512]{3,2,1,0:T(8,128)(2,1)} concatenate(bf16[2,32,4,512]{3,2,1,0:T(4,128)(2,1)} %collective-permute-done, bf16[2,32,6,512]{3,2,1,0:T(8,128)(2,1)} %collective-permute-done.1, bf16[2,32,6,512]{3,2,1,0:T(8,128)(2,1)S(1)} %constant_dynamic-update-slice_fusion, bf16[2,32,6,512]{3,2,1,0:T(8,128)(2,1)} %collective-permute-done.2, ...), dimensions={2} | concatenate | bytes 3407872 | tf_op jit(solution)/shard_map/concatenate | solution.py:39
  64.9 2.8 fusion.43
  67.7 1.9 reshape_squeeze.15
  69.5 1.7 copy.42
  71.2 3.6 %reshape_squeeze.14 = bf16[832,8,64]{2,1,0:T(8,128)(2,1)} reshape(bf16[1,32,26,512]{3,2,1,0:T(8,128)(2,1)} %get-tuple-element.244) | data formatting | bytes 1703936 | tf_op jit(solution)/shard_map/reshape;squeeze | solution.py:108
  74.8 2.9 copy.41
  77.7 61.0 %while.23 = (s32[]{:T(128)}, bf16[8,192,64]{1,2,0:T(8,128)(2,1)}, bf16[8,192,64]{1,2,0:T(8,128)(2,1)}, f32[8,832,64]{1,2,0:T(8,128)}, f32[8,832,64]{1,2,0:T(8,12...) while((s32[]{:T(128)}, bf16[8,192,64]{1,2,0:T(8,128)(2,1)}, ...), condition=%wide.region_4.5_spmd.clone, body=%wide.region_0.4_spmd.clone.sunk | while | flops 126004864 | bytes 5938577 | solution.py:117
  77.7 1.5 fusion.79
  80.8 1.8 fusion.81
  83.6 1.6 fusion.82
  85.3 1.5 fusion.79
  88.4 1.8 fusion.81
  91.3 1.7 fusion.82
  96.1 1.8 fusion.81
  98.9 1.7 fusion.82
  100.5 1.5 fusion.79
  103.7 1.8 fusion.81
  106.5 1.6 fusion.82
  108.1 1.5 fusion.79
  111.3 1.8 fusion.81
  114.1 1.6 fusion.82
  115.8 1.5 fusion.79
  118.9 1.8 fusion.81
  121.8 1.6 fusion.82
  123.4 1.5 fusion.79
  126.5 1.8 fusion.81
  129.4 1.7 fusion.82
  131.0 1.5 fusion.79
  134.2 1.8 fusion.81
  137.0 1.6 fusion.82
  138.7 3.6 %copy.44 = f32[832,8,64]{2,1,0:T(8,128)} copy(f32[832,8,64]{0,2,1:T(8,128)} %bitcast.105) | data formatting | bytes 3407872 | tf_op jit(solution)/shard_map/transpose | solution.py:111
  142.2 4.4 %stack.20 = f32[1,32,26,512]{3,2,1,0:T(8,128)} reshape(f32[832,8,64]{2,1,0:T(8,128)} %copy.44) | data formatting | bytes 3407872 | tf_op jit(solution)/shard_map/stack | solution.py:127
  146.7 2.6 copy.43
  149.3 4.3 %stack.19 = f32[1,32,26,512]{3,2,1,0:T(8,128)} reshape(f32[832,8,64]{2,1,0:T(8,128)} %copy.43) | data formatting | bytes 3407872 | tf_op jit(solution)/shard_map/stack | solution.py:127
  153.6 1.9 constant_dynamic-update-slice_fusion.3
  158.3 4.4 %collective-permute-start.4 = (f32[2,32,6,512]{3,1,2,0:T(8,128)S(1)}, f32[2,32,6,512]{3,1,2,0:T(8,128)}, u32[]{:S(2)}, u32[]{:S(2)}) collective-permute-start(f32[2,32,6,512]{3,1,2,0:T(8,128)S(1)} %copy.45), channel_id=1, source_target_pairs={{0,15},{1,0},{2,1},{3,2},{4,3},{5,4},{6,5},{7,6},{8,7},{9,8},{10,9... | collective-permute-start | bytes 2359304 | tf_op jit(solution)/shard_map/ppermute | solution.py:12
  165.5 2.2 collective-permute-start.7
  167.8 5.4 %collective-permute-done.5 = f32[2,32,6,512]{3,1,2,0:T(8,128)S(1)} collective-permute-done((f32[2,32,6,512]{3,1,2,0:T(8,128)}, f32[2,32,6,512]{3,1,2,0:T(8,128)S(1)}, u32[]{:S(2)}, u32[]{:S(2)}) %collective-permute-start.5) | collective-permute-done | bytes 786464 | tf_op jit(solution)/shard_map/ppermute | solution.py:12
  173.1 4.8 %collective-permute-done.4 = f32[2,32,6,512]{3,1,2,0:T(8,128)} collective-permute-done((f32[2,32,6,512]{3,1,2,0:T(8,128)S(1)}, f32[2,32,6,512]{3,1,2,0:T(8,128)}, u32[]{:S(2)}, u32[]{:S(2)}) %collective-permute-start.4) | collective-permute-done | bytes 786464 | tf_op jit(solution)/shard_map/ppermute | solution.py:12
  177.9 2.6 fusion.36
  180.5 23.0 %collective-permute-done.6 = f32[2,32,4,512]{3,2,1,0:T(4,128)} collective-permute-done((f32[2,32,4,512]{3,2,1,0:T(4,128)}, f32[2,32,4,512]{3,2,1,0:T(4,128)}, u32[]{:S(2)}, u32[]{:S(2)}) %collective-permute-start.6) | collective-permute-done | bytes 524320 | tf_op jit(solution)/shard_map/ppermute | solution.py:12
  204.7 2.2 scatter-add.6
  209.4 2.2 convolution_bitcast_fusion.1
  211.6 3.5 %copy.53 = f32[512,1536]{1,0:T(8,128)} copy(f32[512,1536]{0,1:T(8,128)} %convolution_bitcast_fusion.1) | data formatting | bytes 6291456
  216.7 8.6 %reduce-scatter.5.cloned.1.call-done = f32[512,32]{0,1:T(8,128)} async-done(((f32[512,512]{0,1:T(8,128)}), f32[512,32]{0,1:T(8,128)}) %reduce-scatter.5.cloned.1.call-update) | async-done | bytes 65552 | tf_op jit(solution)/shard_map/reduce_scatter | solution.py:144
  225.3 70.0 %reduce-scatter.7.cloned.1.call-done = f32[32,1536]{1,0:T(8,128)} async-done(((f32[512,1536]{1,0:T(8,128)}), f32[32,1536]{1,0:T(8,128)}) %reduce-scatter.7.cloned.1.call-update) | async-done | bytes 196624
  (129 shorter events, 40.3 us)
Async XLA Ops:
  7.2 1.5 copy-start
  7.2 218.1 %reduce-scatter.5.cloned.1.call-start = ((), (), s32[]{:S(2)}) async-start(), calls=%async_computation.2 | async-start | bytes 1114112 | tf_op jit(solution)/shard_map/reduce_scatter | solution.py:144
  8.7 0.7 copy-start.4
  9.2 9.2 %copy-start.11 = (bf16[32,6,512]{2,0,1:T(8,128)(2,1)S(1)}, bf16[32,6,512]{2,0,1:T(8,128)(2,1)}, u32[]{:S(2)}) copy-start(bf16[32,6,512]{2,0,1:T(8,128)(2,1)} %param.21) | copy-start | bytes 589828
  9.3 9.3 %copy-start.8 = (bf16[512,512]{1,0:T(8,128)(2,1)S(1)}, bf16[512,512]{1,0:T(8,128)(2,1)}, u32[]{:S(2)}) copy-start(bf16[512,512]{1,0:T(8,128)(2,1)} %param.20) | copy-start | bytes 1572868
  9.5 27.1 %collective-permute-start.2 = (bf16[2,32,6,512]{3,2,1,0:T(8,128)(2,1)S(1)}, bf16[2,32,6,512]{3,2,1,0:T(8,128)(2,1)}, u32[]{:S(2)}, u32[]{:S(2)}) collective-permute-start(bf16[2,32,6,512]{3,2,1,0:T(8,128)(2,1)S(1)} %constant_dynamic-update-slice_fusion), channel_id=1, source_target_pairs={{0,15},{1,0},{2,1},{3,2},{4,3},{5,4},{6,5},{7,6},{8,7},{9,8},{10,9... | collective-permute-start | bytes 1179656 | tf_op jit(solution)/shard_map/ppermute | solution.py:12
  15.0 21.7 %collective-permute-start.1 = (bf16[2,32,6,512]{3,2,1,0:T(8,128)(2,1)S(1)}, bf16[2,32,6,512]{3,2,1,0:T(8,128)(2,1)}, u32[]{:S(2)}, u32[]{:S(2)}) collective-permute-start(bf16[2,32,6,512]{3,2,1,0:T(8,128)(2,1)S(1)} %constant_dynamic-update-slice_fusion), channel_id=1, source_target_pairs={{0,1},{1,2},{2,3},{3,4},{4,5},{5,6},{6,7},{7,8},{8,9},{9,10},{10,1... | collective-permute-start | bytes 1179656 | tf_op jit(solution)/shard_map/ppermute | solution.py:12
  16.0 20.6 %collective-permute-start.3 = (bf16[2,32,4,512]{3,2,1,0:T(4,128)(2,1)}, bf16[2,32,4,512]{3,2,1,0:T(4,128)(2,1)}, u32[]{:S(2)}, u32[]{:S(2)}) collective-permute-start(bf16[2,32,4,512]{3,2,1,0:T(4,128)(2,1)} %get-tuple-element.250), channel_id=1, source_target_pairs={{0,14},{1,15},{2,0},{3,1},{4,2},{5,3},{6,4},{7,5},{8,6},{9,7},{10,... | collective-permute-start | bytes 786440 | tf_op jit(solution)/shard_map/ppermute | solution.py:12
  17.0 19.6 %collective-permute-start = (bf16[2,32,4,512]{3,2,1,0:T(4,128)(2,1)}, bf16[2,32,4,512]{3,2,1,0:T(4,128)(2,1)}, u32[]{:S(2)}, u32[]{:S(2)}) collective-permute-start(bf16[2,32,4,512]{3,2,1,0:T(4,128)(2,1)} %get-tuple-element.251), channel_id=1, source_target_pairs={{0,2},{1,3},{2,4},{3,5},{4,6},{5,7},{6,8},{7,9},{8,10},{9,11},{10,... | collective-permute-start | bytes 786440 | tf_op jit(solution)/shard_map/ppermute | solution.py:12
  18.7 18.0 %copy-start.6 = (bf16[192,512]{1,0:T(8,128)(2,1)}, bf16[192,512]{1,0:T(8,128)(2,1)S(1)}, u32[]{:S(2)}) copy-start(bf16[192,512]{1,0:T(8,128)(2,1)S(1)} %reshape.209) | copy-start | bytes 589828
  142.2 4.4 %copy-start.3 = (f32[8,832,64]{1,2,0:T(8,128)S(1)}, f32[8,832,64]{1,2,0:T(8,128)}, u32[]{:S(2)}) copy-start(f32[8,832,64]{1,2,0:T(8,128)} %get-tuple-element.123) | copy-start | bytes 5111812
  153.6 2.2 copy-start.2
  156.1 6.7 %copy-start.1 = (f32[2,32,26,512]{3,2,1,0:T(8,128)}, f32[2,32,26,512]{3,2,1,0:T(8,128)S(1)}, u32[]{:S(2)}) copy-start(f32[2,32,26,512]{3,2,1,0:T(8,128)S(1)} %constant_dynamic-update-slice_fusion.2) | copy-start | bytes 10223620
  156.9 7.2 %copy-start.7 = (bf16[192,512]{1,0:T(8,128)(2,1)S(1)}, bf16[192,512]{1,0:T(8,128)(2,1)}, u32[]{:S(2)}) copy-start(bf16[192,512]{1,0:T(8,128)(2,1)} %copy-done.6) | copy-start | bytes 589828
  156.9 7.2 %copy-start.10 = (bf16[8,192,64]{1,2,0:T(8,128)(2,1)S(1)}, bf16[8,192,64]{1,2,0:T(8,128)(2,1)}, u32[]{:S(2)}) copy-start(bf16[8,192,64]{1,2,0:T(8,128)(2,1)} %get-tuple-element.125) | copy-start | bytes 589828
  158.3 14.8 %collective-permute-start.5 = (f32[2,32,6,512]{3,1,2,0:T(8,128)}, f32[2,32,6,512]{3,1,2,0:T(8,128)S(1)}, u32[]{:S(2)}, u32[]{:S(2)}) collective-permute-start(f32[2,32,6,512]{3,1,2,0:T(8,128)} %copy.47), channel_id=1, source_target_pairs={{0,1},{1,2},{2,3},{3,4},{4,5},{5,6},{6,7},{7,8},{8,9},{9,10},{10,1... | collective-permute-start | bytes 2359304 | tf_op jit(solution)/shard_map/ppermute | solution.py:12
  158.3 19.6 %collective-permute-start.4 = (f32[2,32,6,512]{3,1,2,0:T(8,128)S(1)}, f32[2,32,6,512]{3,1,2,0:T(8,128)}, u32[]{:S(2)}, u32[]{:S(2)}) collective-permute-start(f32[2,32,6,512]{3,1,2,0:T(8,128)S(1)} %copy.45), channel_id=1, source_target_pairs={{0,15},{1,0},{2,1},{3,2},{4,3},{5,4},{6,5},{7,6},{8,7},{9,8},{10,9... | collective-permute-start | bytes 2359304 | tf_op jit(solution)/shard_map/ppermute | solution.py:12
  164.1 39.3 %collective-permute-start.6 = (f32[2,32,4,512]{3,2,1,0:T(4,128)}, f32[2,32,4,512]{3,2,1,0:T(4,128)}, u32[]{:S(2)}, u32[]{:S(2)}) collective-permute-start(f32[2,32,4,512]{3,2,1,0:T(4,128)} %get-tuple-element.240), channel_id=1, source_target_pairs={{0,14},{1,15},{2,0},{3,1},{4,2},{5,3},{6,4},{7,5},{8,6},{9,7},{10,... | collective-permute-start | bytes 1572872 | tf_op jit(solution)/shard_map/ppermute | solution.py:12
  165.5 129.8 %reduce-scatter.7.cloned.1.call-start = ((), (), s32[]{:S(2)}) async-start(), calls=%async_computation.3 | async-start | bytes 3342336
  165.5 41.4 %collective-permute-start.7 = (f32[2,32,4,512]{3,2,1,0:T(4,128)}, f32[2,32,4,512]{3,2,1,0:T(4,128)}, u32[]{:S(2)}, u32[]{:S(2)}) collective-permute-start(f32[2,32,4,512]{3,2,1,0:T(4,128)} %get-tuple-element.239), channel_id=1, source_target_pairs={{0,2},{1,3},{2,4},{3,5},{4,6},{5,7},{6,8},{7,9},{8,10},{9,11},{10,... | collective-permute-start | bytes 1572872 | tf_op jit(solution)/shard_map/ppermute | solution.py:12
  208.3 0.9 copy-start.5
  208.3 1.0 copy-start.9
Sparse Core Ops, SparseCore 0:
  165.6 59.6 reduce-scatter.4
  230.2 65.0 reduce-scatter.6
where the time goes:
time: 305 us; the launch traced here: 302 us
  waiting for transfers between devices  128 us (42%)
  local copies, waits for them, and re-layouts  73.8 us (24%)
  matrix products  63.4 us (21%)
  between operations  14.4 us (5%)
  starting transfers between devices  14.3 us (5%)
  other arithmetic  7.7 us (3%)
    unnamed x3, waiting for transfers between devices  70 us
    ppermute x8, waiting for transfers between devices, from_behind(): lax.ppermute(array, axis, [(i, (i + by) % size) for i in range(size)])  49.7 us
    concatenate x1, local copies, waits for them, and re-layouts, reach(): return jnp.concatenate(left_parts + [block] + right_parts, axis=2)  28.2 us
    dot_general x18, matrix products, contract_first(): lax.dot_general(left_side, right_side, (((0,), (0,)), ((), ())), preferre...  24.8 us
    dot_general x18, matrix products, contract_rows(): lax.dot_general(left_side, right_side, (((1,), (1,)), ((), ())), preferre...  15.6 us
    dot_general x8, matrix products, attend(): jnp.dot(grad_score, key_head, preferred_element_type=jnp.float32)  14.6 us
    ppermute x8, starting transfers between devices, from_behind(): lax.ppermute(array, axis, [(i, (i + by) % size) for i in range(size)])  14.2 us
    unnamed x32, local copies, waits for them, and re-layouts  13.2 us
  transfers between devices with their start and end apart: 10, of which 6 were waited for; matrix products, arithmetic and copies ran while one was open for 7% of the time, Pallas kernels for 0%

commit v1 on v0

v1 whole, which is shorter than its diff:
```python
import functools

import jax
import jax.numpy as jnp
from jax import lax
from jax.experimental import pallas as pl
from jax.experimental.pallas import tpu as pltpu
from jax.sharding import PartitionSpec as P

HEADS = 8
RADIUS = 10
F32 = jnp.float32
LOW = jnp.bfloat16


def rim_widths(cols):
    hop_count = (RADIUS + cols - 1) // cols
    return [min(cols, RADIUS - (distance - 1) * cols) for distance in range(1, hop_count + 1)]


def segments(cols):
    parts = []
    for distance, count in enumerate(rim_widths(cols), 1):
        parts.append((-distance, count, -(distance - 1) * cols - count, cols - count))
        parts.append((distance, count, distance * cols, 0))
    return parts


def nn(left, right):
    return lax.dot_general(left, right, (((1,), (0,)), ((), ())), preferred_element_type=F32)


def nt(left, right):
    return lax.dot_general(left, right, (((1,), (1,)), ((), ())), preferred_element_type=F32)


def tn(left, right):
    return lax.dot_general(left, right, (((0,), (0,)), ((), ())), preferred_element_type=F32)


def kernel(
    n, lat, cols, staged, x_ref, u_ref, wi_ref, wo_ref, *refs
):
    if staged:
        tg_ref, ig_ref, og_ref = refs[:3]
        refs = refs[3:]
    else:
        tg_ref, term_ref = refs[:2]
        refs = refs[2:]
    xe, xet, ut, kv, qs, gs, dq, dkv, bias, tgs, tgr = refs[:11]
    hs, hr, bs, br = refs[11:15]
    own = lat * cols
    width = x_ref.shape[1]
    parts = segments(cols)
    me = lax.axis_index("lon")
    pairs = width // 128
    half = 64
    scale = half ** (-0.5)

    def at(offset):
        return lax.rem(me + offset + n, n)

    offsets = [part[0] for part in parts]
    if staged:
        tb, ra, sa, rb, sb, rc, sas, sar, sbs, sbr, scs, scr = refs[15:]
        deep = n // 4
        core = lax.rem(me, 2)
        mid = lax.rem(me // 2, 2)
        top = me // 4
        offsets = offsets + [4 * k for k in range(1, deep)]
    barrier = pltpu.get_barrier_semaphore()
    for offset in offsets:
        pl.semaphore_signal(
            barrier, inc=1, device_id={"lon": at(offset)}, device_id_type=pl.DeviceIdType.MESH
        )
    pl.semaphore_wait(barrier, len(offsets))

    def remote(src, dst, send, recv, target):
        return pltpu.make_async_remote_copy(
            src_ref=src,
            dst_ref=dst,
            send_sem=send,
            recv_sem=recv,
            device_id={"lon": target},
            device_id_type=pl.DeviceIdType.MESH,
        )

    halo = []
    start = own
    starts = []
    for index, (hop, count, _, first) in enumerate(parts):
        halo.append(
            remote(
                x_ref.at[pl.ds(first * lat, count * lat)],
                xe.at[pl.ds(start, count * lat)],
                hs.at[index],
                hr.at[index],
                at(-hop),
            )
        )
        starts.append(start)
        start += count * lat
    total = start
    for copy in halo:
        copy.start()

    x_own = x_ref[...]
    xe[0:own, :] = x_own
    qs[...] = (nn(x_own, wi_ref[:, 0:width]).astype(LOW).astype(F32) * scale).astype(LOW)
    gs[...] = nt(u_ref[...], wo_ref[...]).astype(LOW)
    ut[...] = u_ref[...].T
    kv[0:own, :] = nn(x_own, wi_ref[:, width:]).astype(LOW)

    rows2 = lax.broadcasted_iota(jnp.int32, (2 * own, total), 0)
    keys2 = lax.broadcasted_iota(jnp.int32, (2 * own, total), 1)
    rows2 = jnp.where(rows2 >= own, rows2 - own, rows2)
    tile = lax.div(keys2, lat)
    place = tile
    count_before = cols
    for hop, count, first, _ in parts:
        place = jnp.where(tile >= count_before, tile + (first - count_before), place)
        count_before += count
    near_col = jnp.abs(lax.div(rows2, lat) - place) <= RADIUS
    near_lat = jnp.abs(lax.rem(rows2, lat) - lax.rem(keys2, lat)) <= RADIUS
    bias[...] = jnp.where(near_col & near_lat, 0.0, -1e30).astype(F32)

    for copy in halo:
        copy.wait()
    kv[own:total, :] = nn(xe[own:total, :], wi_ref[:, width:]).astype(LOW)
    xet[...] = xe[...].T

    if staged:

        def copy_a(p):
            return remote(
                tb.at[p, 1 - core], ra.at[p], sas.at[p], sar.at[p], me + 1 - 2 * core
            )

        def copy_b(p):
            return remote(
                sa.at[p, 1 - mid], rb.at[p], sbs.at[p], sbr.at[p], me + 2 - 4 * mid
            )

        def copies_c(p):
            out = []
            for k in range(1, deep):
                target = lax.rem(top + k, deep)
                out.append(
                    remote(
                        sb.at[p, target],
                        rc.at[p, k - 1],
                        scs.at[p, k - 1],
                        scr.at[p, k - 1],
                        target * 4 + lax.rem(me, 4),
                    )
                )
            return out

        def stage_b(p):
            copy_a(p).wait()
            mine = tb[p, core].astype(F32) + ra[p].astype(F32)
            sa[p] = mine.astype(LOW).reshape(sa.shape[1:])
            copy_b(p).start()

        def stage_c(p):
            copy_b(p).wait()
            sb[p] = (sa[p, mid].astype(F32) + rb[p].astype(F32)).astype(LOW)
            for copy in copies_c(p):
                copy.start()

        def finish(p):
            for copy in copies_c(p):
                copy.wait()
            done = sa[p, mid, top].astype(F32) + rb[p, top].astype(F32)
            for k in range(1, deep):
                done = done + rc[p, k - 1].astype(F32)
            for k in range(3):
                ig_ref[:, width * k + 128 * p : width * k + 128 * p + 128] = done[
                    :, 128 * k : 128 * k + 128
                ]
            og_ref[:, 128 * p : 128 * p + 128] = done[:, 384:512]

    lane = lax.broadcasted_iota(jnp.int32, (own, 128), 1)

    def stacked(block):
        zero = jnp.zeros_like(block)
        return jnp.concatenate(
            [jnp.where(lane < half, block, zero), jnp.where(lane < half, zero, block)], axis=0
        )

    def picked(block):
        return jnp.where(lane < half, block[0:own], block[own : 2 * own])

    def pair(p, carry):
        here = pl.ds(pl.multiple_of(p * 128, 128), 128)
        there = pl.ds(pl.multiple_of(width + p * 128, 128), 128)
        q2 = stacked(qs[:, here])
        g2 = stacked(gs[:, here])
        k2 = kv[:, here]
        v2 = kv[:, there]
        score = nt(q2, k2) + bias[...]
        peak = jnp.max(score, axis=1, keepdims=True)
        grown = jnp.exp(score - peak)
        probs = grown * (1.0 / jnp.sum(grown, axis=1, keepdims=True))
        low = probs.astype(LOW)
        reached = nn(low, v2).astype(LOW)
        delta = jnp.sum(g2.astype(F32) * reached.astype(F32), axis=1, keepdims=True)
        slope = (probs * (nt(g2, v2) - delta)).astype(LOW)
        dq_p = (picked(nn(slope, k2)) * scale).astype(LOW)
        att_p = picked(reached)
        dk_p = tn(q2, slope).T.astype(LOW)
        dv_p = tn(g2, low).T.astype(LOW)
        dq[:, here] = dq_p
        dkv[:, here] = dk_p
        dkv[:, there] = dv_p
        term_q = nn(xet[:, 0:own], dq_p)
        term_k = nn(xet[...], dk_p)
        term_v = nn(xet[...], dv_p)
        term_o = nn(ut[...], att_p)
        terms = (term_q, term_k, term_v, term_o)
        if staged:
            rows = width // n
            for k, term in enumerate(terms):
                block = term.astype(LOW)
                for j in range(n):
                    tb[p, j % 2, ((j // 2) % 2) * deep + j // 4, :, 128 * k : 128 * k + 128] = (
                        block[rows * j : rows * j + rows]
                    )
            copy_a(p).start()

            @pl.when(p >= 1)
            def _():
                stage_b(p - 1)

            @pl.when(p >= 2)
            def _():
                stage_c(p - 2)
        else:
            for k, term in enumerate(terms):
                term_ref[:, pl.ds(pl.multiple_of(width * k + p * 128, 128), 128)] = term
        return carry

    lax.fori_loop(0, pairs, pair, 0)

    tgs[...] = nt(dkv[own:total, :], wi_ref[:, width:]).astype(LOW)
    back = []
    start = 0
    for index, (hop, count, _, first) in enumerate(parts):
        back.append(
            remote(
                tgs.at[pl.ds(start, count * lat)],
                tgr.at[pl.ds(start, count * lat)],
                bs.at[index],
                br.at[index],
                at(hop),
            )
        )
        start += count * lat
    for copy in back:
        copy.start()
    if staged:
        stage_b(pairs - 1)
        stage_c(pairs - 2)
    mine = nt(dkv[0:own, :], wi_ref[:, width:]) + nt(dq[...], wi_ref[:, 0:width])
    bias[0:own, 0:width] = mine
    if staged:
        stage_c(pairs - 1)
    for copy in back:
        copy.wait()
    start = 0
    for index, (hop, count, _, first) in enumerate(parts):
        spot = slice(first * lat, (first + count) * lat)
        bias[spot, 0:width] += tgr[start : start + count * lat, :].astype(F32)
        start += count * lat
    tg_ref[...] = bias[0:own, 0:width].astype(LOW)
    if staged:
        for p in range(pairs):
            finish(p)


def body(n, tokens, input_weight, output_weight, upstream):
    lat, cols, width = tokens.shape
    own = lat * cols
    parts = segments(cols)
    rim = lat * sum(part[1] for part in parts)
    total = own + rim
    rows = width // n
    staged = rows % 16 == 0 and n % 4 == 0 and n > 8
    x = tokens.transpose(1, 0, 2).reshape(own, width)
    u = upstream.transpose(1, 0, 2).reshape(own, width)
    pairs = width // 128
    vmem = pl.BlockSpec(memory_space=pltpu.VMEM)
    out_shape = [jax.ShapeDtypeStruct((own, width), LOW)]
    scratch = [
        pltpu.VMEM((total, width), LOW),
        pltpu.VMEM((width, total), LOW),
        pltpu.VMEM((width, own), LOW),
        pltpu.VMEM((total, 2 * width), LOW),
        pltpu.VMEM((own, width), LOW),
        pltpu.VMEM((own, width), LOW),
        pltpu.VMEM((own, width), LOW),
        pltpu.VMEM((total, 2 * width), LOW),
        pltpu.VMEM((2 * own, total), F32),
        pltpu.VMEM((rim, width), LOW),
        pltpu.VMEM((rim, width), LOW),
    ] + [pltpu.SemaphoreType.DMA((len(parts),))] * 4
    if staged:
        deep = n // 4
        out_shape += [
            jax.ShapeDtypeStruct((rows, 3 * width), F32),
            jax.ShapeDtypeStruct((rows, width), F32),
        ]
        scratch += [
            pltpu.VMEM((pairs, 2, 2 * deep, rows, 512), LOW),
            pltpu.VMEM((pairs, 2 * deep, rows, 512), LOW),
            pltpu.VMEM((pairs, 2, deep, rows, 512), LOW),
            pltpu.VMEM((pairs, deep, rows, 512), LOW),
            pltpu.VMEM((pairs, deep, rows, 512), LOW),
            pltpu.VMEM((pairs, deep - 1, rows, 512), LOW),
        ]
        scratch += [pltpu.SemaphoreType.DMA((pairs,))] * 4
        scratch += [pltpu.SemaphoreType.DMA((pairs, deep - 1))] * 2
    else:
        out_shape += [jax.ShapeDtypeStruct((width, 4 * width), F32)]
    results = pl.pallas_call(
        functools.partial(kernel, n, lat, cols, staged),
        out_shape=out_shape,
        in_specs=[vmem] * 4,
        out_specs=[vmem] * len(out_shape),
        scratch_shapes=scratch,
        compiler_params=pltpu.CompilerParams(
            collective_id=0, has_side_effects=True, vmem_limit_bytes=56 * 1024 * 1024
        ),
    )(x, u, input_weight, output_weight)
    token_grads = results[0].reshape(cols, lat, width).transpose(1, 0, 2)
    if staged:
        return token_grads, results[1], results[2].T
    term = results[1]
    input_grads = lax.psum_scatter(term[:, : 3 * width], "lon", scatter_dimension=0, tiled=True)
    output_grads = lax.psum_scatter(term[:, 3 * width :].T, "lon", scatter_dimension=1, tiled=True)
    return token_grads, input_grads, output_grads


def solution(mesh):
    in_specs = (P("groups", "lon", None), P(), P(), P("groups", "lon", None))
    out_specs = (P("groups", "lon", None), P("lon", "groups"), P("groups", "lon"))
    return jax.shard_map(
        functools.partial(body, mesh.shape["lon"]),
        mesh=mesh,
        in_specs=in_specs,
        out_specs=out_specs,
        check_vma=False,
    )
```

time: 305 us -> 57.8 us (0.19)
  waiting for transfers between devices: 128 us -> 0 us
  local copies, waits for them, and re-layouts: 73.8 us -> 4.71 us
  matrix products: 63.4 us -> 0 us
  Pallas kernels: 0 us -> 52.2 us
  starting transfers between devices: 14.3 us -> 0 us
  between operations: 14.4 us -> 0.64 us
  other arithmetic: 7.7 us -> 0 us
    unnamed x3 -> x0, waiting for transfers between devices: 70 us -> none
    dot_general x53 -> x0, matrix products: 63.4 us -> none  [the longest x18 24.8 us: contract_first(): lax.dot_general(left_side, right_side, (((0,), (0,)), ((), ())), preferre...]
    pallas_call x0 -> x1, Pallas kernels: none -> 52.2 us  [body(): pl.pallas_call(functools.partial(kernel, n, lat, cols, staged), out_shape...]
    ppermute x8 -> x0, waiting for transfers between devices: 49.7 us -> none  [from_behind(): lax.ppermute(array, axis, [(i, (i + by) % size) for i in range(size)])]
    concatenate x1 -> x0, local copies, waits for them, and re-layouts: 28.2 us -> none  [reach(): return jnp.concatenate(left_parts + [block] + right_parts, axis=2)]
    another operation x13 -> x0, local copies, waits for them, and re-layouts: 15 us -> none  [the longest x3 8.97 us: body(): jnp.stack([join_heads(grad_key_ext), join_heads(grad_value_ext)])]
    ppermute x8 -> x0, starting transfers between devices: 14.2 us -> none  [from_behind(): lax.ppermute(array, axis, [(i, (i + by) % size) for i in range(size)])]
    reduce_scatter x1 -> x0, waiting for transfers between devices: 8.63 us -> none  [body(): lax.psum_scatter(term_output, 'lon', scatter_dimension=1, tiled=True)]
  transfers between devices with their start and end apart: 10 -> 0, of which waited for: 6 -> 0; matrix products, arithmetic and copies ran while one was open for 7% -> 0% of each run, Pallas kernels for 0% -> 0%
where the time goes in v1:
time: 57.8 us; the launch traced here: 57.6 us
  Pallas kernels  52.2 us (90%)
  local copies, waits for them, and re-layouts  4.71 us (8%)
  between operations  0.64 us (1%)
    pallas_call x1, Pallas kernels, body(): pl.pallas_call(functools.partial(kernel, n, lat, cols, staged), out_shape...  52.2 us
    unnamed x3, local copies, waits for them, and re-layouts  4.71 us

profile of v1, /device:TPU:0, one launch (start us, length us, event | category | flops | bytes accessed | tf_op | source)
XLA Modules:
  0.0 57.6 jit_solution(9244905538223663696)
XLA Ops:
  0.6 52.2 %shard_map.67 = (bf16[192,512]{1,0:T(8,128)(2,1)}, f32[32,1536]{1,0:T(8,128)}, f32[32,512]{1,0:T(8,128)}) custom-call(bf16[192,512]{1,0:T(8,128)(2,1)} %bitcast.10, bf16[192,512]{1,0:T(8,128)(2,1)} %bitcast.11, bf16[512,1536]{1,0:T(8,128)(2,1)} %wi_ref.1, bf16[512,512]{1,0:T(8,128)(2,1)} %wo_ref.1), custom_call_target="tpu_custom_call" | custom-call | tf_op jit(solution)/shard_map/pallas_call | solution.py:325
  52.9 1.6 %copy.10 = bf16[32,6,512]{2,0,1:T(8,128)(2,1)} copy(bf16[32,6,512]{2,0,1:T(8,128)(2,1)} %bitcast.12) | data formatting | bytes 393216
  54.5 1.6 %copy.11 = f32[32,1536]{1,0:T(8,128)} copy(f32[32,1536]{1,0:T(8,128)} %get-tuple-element.13) | data formatting | bytes 393216
  56.1 1.5 %copy.12 = f32[512,32]{0,1:T(8,128)} copy(f32[512,32]{0,1:T(8,128)} %bitcast.13) | data formatting | bytes 131072

commit v2 on v1

--- a/solution.py
+++ b/solution.py
@@ -85,22 +85,30 @@
             device_id_type=pl.DeviceIdType.MESH,
         )
 
-    halo = []
-    start = own
-    starts = []
-    for index, (hop, count, _, first) in enumerate(parts):
-        halo.append(
-            remote(
-                x_ref.at[pl.ds(first * lat, count * lat)],
-                xe.at[pl.ds(start, count * lat)],
-                hs.at[index],
-                hr.at[index],
-                at(-hop),
-            )
-        )
-        starts.append(start)
-        start += count * lat
-    total = start
+    near, far = cols * lat, parts[2][1] * lat
+    left1, right1, left2, right2 = own, own + near, own + 2 * near, own + 2 * near + far
+    total = right2 + far
+    side = lax.rem(me, 2)
+    sibling = me + 1 - 2 * side
+    across = at(2 - 4 * side)
+    across_back = at(4 * side - 2)
+
+    def rows_at(first, count):
+        return pl.ds(pl.multiple_of(first, 32), count)
+
+    far2 = left2 + side * far
+    given = left1 + (near - far) * (1 - side) + near * side
+    halo = [
+        remote(x_ref, xe.at[pl.ds(left1, near)], hs.at[0], hr.at[0], at(1)),
+        remote(x_ref, xe.at[pl.ds(right1, near)], hs.at[1], hr.at[1], at(-1)),
+        remote(
+            x_ref.at[rows_at((near - far) * (1 - side), far)],
+            xe.at[rows_at(far2, far)],
+            hs.at[2],
+            hr.at[2],
+            across,
+        ),
+    ]
     for copy in halo:
         copy.start()
 
@@ -124,8 +132,24 @@
     near_lat = jnp.abs(lax.rem(rows2, lat) - lax.rem(keys2, lat)) <= RADIUS
     bias[...] = jnp.where(near_col & near_lat, 0.0, -1e30).astype(F32)
 
-    for copy in halo:
-        copy.wait()
+    remote(
+        x_ref, xe.at[rows_at(left1 + near * side, near)], hs.at[side], hr.at[side], at(1 - 2 * side)
+    ).wait_recv()
+    hand_on = remote(
+        xe.at[rows_at(given, far)], xe.at[rows_at(far2, far)], hs.at[3], hr.at[3], sibling
+    )
+    hand_on.start()
+    remote(
+        x_ref,
+        xe.at[rows_at(left1 + near * (1 - side), near)],
+        hs.at[1 - side],
+        hr.at[1 - side],
+        at(2 * side - 1),
+    ).wait_recv()
+    halo[0].wait_send()
+    halo[1].wait_send()
+    halo[2].wait()
+    hand_on.wait()
     kv[own:total, :] = nn(xe[own:total, :], wi_ref[:, width:]).astype(LOW)
     xet[...] = xe[...].T
 
@@ -242,40 +266,58 @@
 
     lax.fori_loop(0, pairs, pair, 0)
 
-    tgs[...] = nt(dkv[own:total, :], wi_ref[:, width:]).astype(LOW)
-    back = []
-    start = 0
-    for index, (hop, count, _, first) in enumerate(parts):
-        back.append(
-            remote(
-                tgs.at[pl.ds(start, count * lat)],
-                tgr.at[pl.ds(start, count * lat)],
-                bs.at[index],
-                br.at[index],
-                at(hop),
-            )
-        )
-        start += count * lat
+    handed = left2 + (1 - side) * far
+    tgs[2 * near : 2 * near + far, :] = nt(dkv[rows_at(handed, far), :], wi_ref[:, width:]).astype(LOW)
+    hand_back = remote(
+        tgs.at[pl.ds(2 * near, far)], tgr.at[pl.ds(2 * near, far)], bs.at[3], br.at[3], sibling
+    )
+    hand_back.start()
+    bias[0 : 2 * near, 0:width] = nt(dkv[left1:left2, :], wi_ref[:, width:])
+    tgs[2 * near + far : 2 * near + 2 * far, :] = nt(
+        dkv[rows_at(far2, far), :], wi_ref[:, width:]
+    ).astype(LOW)
+    if staged:
+        stage_b(pairs - 1)
+    cross = remote(
+        tgs.at[pl.ds(2 * near + far, far)],
+        tgr.at[pl.ds(2 * near + far, far)],
+        bs.at[2],
+        br.at[2],
+        across_back,
+    )
+    cross.start()
+    hand_back.wait()
+    bias[rows_at(given - own, far), 0:width] += tgr[2 * near : 2 * near + far, :].astype(F32)
+    tgs[0 : 2 * near, :] = bias[0 : 2 * near, 0:width].astype(LOW)
+    back = [
+        remote(tgs.at[pl.ds(0, near)], tgr.at[pl.ds(0, near)], bs.at[0], br.at[0], at(-1)),
+        remote(tgs.at[pl.ds(near, near)], tgr.at[pl.ds(near, near)], bs.at[1], br.at[1], at(1)),
+    ]
     for copy in back:
         copy.start()
     if staged:
-        stage_b(pairs - 1)
         stage_c(pairs - 2)
     mine = nt(dkv[0:own, :], wi_ref[:, width:]) + nt(dq[...], wi_ref[:, 0:width])
     bias[0:own, 0:width] = mine
     if staged:
         stage_c(pairs - 1)
+    cross.wait()
+    bias[rows_at((near - far) * (1 - side), far), 0:width] += tgr[
+        2 * near + far : 2 * near + 2 * far, :
+    ].astype(F32)
     for copy in back:
         copy.wait()
-    start = 0
-    for index, (hop, count, _, first) in enumerate(parts):
-        spot = slice(first * lat, (first + count) * lat)
-        bias[spot, 0:width] += tgr[start : start + count * lat, :].astype(F32)
-        start += count * lat
+    bias[0:own, 0:width] += tgr[0:near, :].astype(F32) + tgr[near : 2 * near, :].astype(F32)
     tg_ref[...] = bias[0:own, 0:width].astype(LOW)
     if staged:
         for p in range(pairs):
             finish(p)
+
+
+def place(tg_ref, ig_ref, og_ref, tg_out, ig_out, og_out):
+    tg_out[...] = tg_ref[...]
+    ig_out[...] = ig_ref[...]
+    og_out[...] = og_ref[...]
 
 
 def body(n, tokens, input_weight, output_weight, upstream):
@@ -332,6 +374,17 @@
             collective_id=0, has_side_effects=True, vmem_limit_bytes=56 * 1024 * 1024
         ),
     )(x, u, input_weight, output_weight)
+    if staged:
+        results = pl.pallas_call(
+            place,
+            out_shape=[
+                jax.ShapeDtypeStruct((own, width), LOW),
+                jax.ShapeDtypeStruct((rows, 3 * width), F32),
+                jax.ShapeDtypeStruct((rows, width), F32),
+            ],
+            in_specs=[vmem] * 3,
+            out_specs=[vmem] * 3,
+        )(*results)
     token_grads = results[0].reshape(cols, lat, width).transpose(1, 0, 2)
     if staged:
         return token_grads, results[1], results[2].T

time: 57.8 us -> 47.2 us (0.82)
  Pallas kernels: 52.2 us -> 46.4 us
  local copies, waits for them, and re-layouts: 4.71 us -> 0 us
    pallas_call x1, Pallas kernels: 52.2 us -> 44.6 us  [body(): pl.pallas_call(functools.partial(kernel, n, lat, cols, staged), out_shape...]
    unnamed x3 -> x0, local copies, waits for them, and re-layouts: 4.71 us -> none
    pallas_call x0 -> x1, Pallas kernels: none -> 1.8 us  [body(): pl.pallas_call(place, out_shape=[jax.ShapeDtypeStruct((own, width), LOW),...]
where the time goes in v2:
time: 47.2 us; the launch traced here: 47 us
  Pallas kernels  46.4 us (98%)
  between operations  0.64 us (1%)
    pallas_call x1, Pallas kernels, body(): pl.pallas_call(functools.partial(kernel, n, lat, cols, staged), out_shape...  44.6 us
    pallas_call x1, Pallas kernels, body(): pl.pallas_call(place, out_shape=[jax.ShapeDtypeStruct((own, width), LOW),...  1.8 us

profile of v2, /device:TPU:0, one launch (start us, length us, event | category | flops | bytes accessed | tf_op | source)
XLA Modules:
  0.0 47.0 jit_solution(257780598092442219)
XLA Ops:
  0.6 44.6 %shard_map.67 = (bf16[192,512]{1,0:T(8,128)(2,1)}, f32[32,1536]{1,0:T(8,128)}, f32[32,512]{1,0:T(8,128)}) custom-call(bf16[192,512]{1,0:T(8,128)(2,1)} %bitcast.10, bf16[192,512]{1,0:T(8,128)(2,1)} %bitcast.11, bf16[512,1536]{1,0:T(8,128)(2,1)} %wi_ref.1, bf16[512,512]{1,0:T(8,128)(2,1)} %wo_ref.1), custom_call_target="tpu_custom_call" | custom-call | tf_op jit(solution)/shard_map/pallas_call | solution.py:367
  45.2 1.8 %shard_map.68 = (bf16[192,512]{1,0:T(8,128)(2,1)}, f32[32,1536]{1,0:T(8,128)}, f32[32,512]{1,0:T(8,128)}) custom-call(bf16[192,512]{1,0:T(8,128)(2,1)} %get-tuple-element.9.tg_ref, f32[32,1536]{1,0:T(8,128)} %get-tuple-element.10.ig_ref, f32[32,512]{1,0:T(8,128)} %get-tuple-element.11.og_ref), custom_call_target="tpu_custom_call" | custom-call | tf_op jit(solution)/shard_map/pallas_call | solution.py:378
